TPU v7x, 128 devices: a whole 4x4x4 slice. The times are simulated.
128 devices in a mesh: user: 16 (over x, y_lo, core), cand: 8 (over z, y_hi).
Axes of the slice: x: 4, y: 4 (y_hi: 2, y_lo: 2; y = y_hi * 2 + y_lo), z: 4, core: 2. Of those that a mesh axis runs over, the one named last changes fastest.
Arguments:
- pooled: bfloat16 [16, 32, 1024, 1024], P('user', None, 'cand'), may hold values from -6 to 6
- cand_feats: bfloat16 [65536, 1024], P(('user', 'cand')), may hold values from -6 to 6
- hist_len: int32 [32], P('user'), may hold values from 1 to 1024, 16384 in all
- cand_user: int32 [65536], P(('user', 'cand')), may hold values from 0 to 31, as said below
- w_in: bfloat16 [1024, 4096], replicated, may hold values from -0.1875 to 0.1875
- w_out: bfloat16 [1024, 1024], replicated, may hold values from -0.1875 to 0.1875
Outputs:
- hist_out: bfloat16 [32, 1024, 1024], P('user', 'cand')
- cand_out: bfloat16 [65536, 1024], P(('user', 'cand'))
Inputs may be any that keep to these rules, and one draw needn't show every extreme that they name: `hist_len`: the lengths sum to 16384, and the longest is 1024. `cand_user`: candidate row r belongs to one of the 2 users numbered from (r // 4096) * 2 on.
All inputs are finite; a program needn't handle non-finite values. No bound on the sum of `hist_len` on one device may be relied on, other than what follows from the above.
Results may differ from a plain program's by a relative error of at most 0.022.
Values may be sent and summed in bfloat16 or wider, within the bound.
No kernel may reach another device: no remote copies, remote signals or barrier semaphores. Data moves between devices by JAX's collectives and lax.ppermute only.
A program may use at most 128 MiB of HBM per device.

v0:
```python
import jax
import jax.numpy as jnp
from jax import lax
from jax.sharding import PartitionSpec as P

H = 8


def layer_norm(rows):
    mean = jnp.mean(rows, axis=-1, keepdims=True)
    centered = rows - mean
    var = jnp.mean(centered * centered, axis=-1, keepdims=True)
    return centered * lax.rsqrt(var + 1e-05)


def project(feats, w_in):
    proj = jax.nn.silu(jnp.dot(feats, w_in, preferred_element_type=jnp.float32))
    width = w_in.shape[0]
    return tuple((proj[:, j * width : (j + 1) * width].astype(jnp.bfloat16) for j in range(4)))


def to_heads(block, heads):
    shape = block.shape
    width = shape[-1]
    split = block.reshape(shape[:-1] + (heads, width // heads))
    order = (len(shape) - 1,) + tuple(range(len(shape) - 1))
    return jnp.transpose(split, order + (len(shape),))


def finish(summed, upart, feats, w_out):
    mixed = (layer_norm(summed) * upart.astype(jnp.float32)).astype(jnp.bfloat16)
    return jnp.dot(mixed, w_out, preferred_element_type=jnp.float32) + feats.astype(jnp.float32)


def local(pooled, cand_feats, hist_len, cand_user, w_in, w_out):
    users_dev = hist_len.shape[0]
    width = w_out.shape[0]
    heads = H
    head_size = width // heads
    scale = 1.0 / jnp.sqrt(jnp.float32(head_size))
    x_hist = layer_norm(
        jnp.sum(
            lax.all_to_all(pooled, "user", split_axis=1, concat_axis=0, tiled=True),
            axis=0,
            dtype=jnp.float32,
        )
    ).astype(jnp.bfloat16)
    slots = x_hist.shape[1]
    hist_rows = x_hist.reshape(users_dev * slots, width)
    u_hist, v_hist, q_hist, k_hist = project(hist_rows, w_in)
    x_cand = layer_norm(cand_feats.astype(jnp.float32)).astype(jnp.bfloat16)
    u_cand, v_cand, q_cand, k_cand = project(x_cand, w_in)
    cand_rows = x_cand.shape[0]
    owners = cand_user - lax.axis_index("user") * users_dev
    q_pos = lax.axis_index("cand") * slots + jnp.arange(slots, dtype=jnp.int32)
    qh_heads = to_heads(q_hist.reshape(users_dev, slots, width), heads)
    qc_heads = to_heads(q_cand, heads)
    keys_piece = lax.all_gather(k_hist.reshape(users_dev, slots, width), "cand", axis=1, tiled=True)
    count = keys_piece.shape[1]
    k_pos = jnp.arange(count, dtype=jnp.int32)
    hist_mask = (k_pos[None, None, :] <= q_pos[None, :, None]) & (
        k_pos[None, None, :] < hist_len[:, None, None]
    )
    flat = jnp.arange(users_dev * count, dtype=jnp.int32)
    key_user = flat // count
    live = flat % count < hist_len[key_user]
    cand_mask = (owners[:, None] == key_user[None, :]) & live[None, :]
    k_heads = to_heads(keys_piece, heads)
    v_heads = to_heads(
        lax.all_gather(v_hist.reshape(users_dev, slots, width), "cand", axis=1, tiled=True), heads
    )

    def one_head(operands):
        query_h, query_c, key_h, value_h = operands
        scores = (
            jnp.einsum("uqd,ukd->uqk", query_h, key_h, preferred_element_type=jnp.float32) * scale
        )
        weights = jnp.where(hist_mask, jax.nn.silu(scores), 0.0).astype(jnp.bfloat16)
        part_hist = jnp.einsum("uqk,ukd->uqd", weights, value_h, preferred_element_type=jnp.float32)
        key_flat = key_h.reshape(users_dev * count, head_size)
        value_flat = value_h.reshape(users_dev * count, head_size)
        scores_c = (
            jnp.einsum("cd,kd->ck", query_c, key_flat, preferred_element_type=jnp.float32) * scale
        )
        weights_c = jnp.where(cand_mask, jax.nn.silu(scores_c), 0.0).astype(jnp.bfloat16)
        part_cand = jnp.dot(weights_c, value_flat, preferred_element_type=jnp.float32)
        return (part_hist, part_cand)

    part_hist, part_cand = lax.map(one_head, (qh_heads, qc_heads, k_heads, v_heads))
    hist_sum = part_hist
    cand_sum = part_cand
    hist_sum = jnp.transpose(hist_sum, (1, 2, 0, 3)).reshape(users_dev * slots, width)
    cand_sum = jnp.transpose(cand_sum, (1, 0, 2))
    own = (
        (q_cand.astype(jnp.float32) * k_cand.astype(jnp.float32))
        .reshape(cand_rows, heads, head_size)
        .sum(-1)
    )
    own = jax.nn.silu(own * scale).astype(jnp.bfloat16).astype(jnp.float32)
    cand_sum = cand_sum + own[:, :, None] * v_cand.reshape(cand_rows, heads, head_size).astype(
        jnp.float32
    )
    cand_out = finish(cand_sum.reshape(cand_rows, width), u_cand, x_cand, w_out).astype(
        jnp.bfloat16
    )
    hist_res = finish(hist_sum, u_hist, hist_rows, w_out).reshape(users_dev, slots, width)
    keep = q_pos[None, :, None] < hist_len[:, None, None]
    hist_out = jnp.where(keep, hist_res, 0.0).astype(jnp.bfloat16)
    return (hist_out, cand_out)


def solution(mesh):
    placed = (
        P("user", None, "cand", None),
        P(("user", "cand"), None),
        P("user"),
        P(("user", "cand")),
        P(),
        P(),
    )
    return jax.shard_map(
        local,
        mesh=mesh,
        in_specs=placed,
        out_specs=(P("user", "cand", None), P(("user", "cand"), None)),
        check_vma=False,
    )
```

profile of v0, /device:TPU:0, one launch (start us, length us, event | category | flops | bytes accessed | tf_op | source)
XLA Modules:
  0.0 366.2 jit_solution(18052631554689522488)
XLA Ops:
  7.2 100.9 %all_to_all.4 = bf16[1,32,128,1024]{3,2,0,1:T(8,128)(2,1)} all-to-all(bf16[1,32,128,1024]{3,2,0,1:T(8,128)(2,1)} %bitcast.144), channel_id=1, replica_groups=mesh['user'=16,'cand'=8] {'user'}, dimensions={1} | all-to-all | bytes 16777216 | tf_op jit(solution)/shard_map/all_to_all | solution.py:43
  108.1 5.5 %reduce_sum.99 = f32[2,128,1024]{2,1,0:T(8,128)S(1)} reduce(bf16[16,2,128,1024]{3,2,1,0:T(8,128)(2,1)} %bitcast.139, f32[]{:T(128)} %constant.91.clone.1), dimensions={0}, to_apply=%region_0.0 | reduce | flops 3932160 | bytes 9437188 | tf_op jit(solution)/shard_map/reduce_sum | solution.py:42
  113.6 4.5 %convert_reduce_fusion = f32[32,128]{1,0:T(8,128)S(1)} fusion(bf16[1,32,128,1024]{3,2,0,1:T(8,128)(2,1)} %all_to_all.4), kind=kLoop, calls=%fused_computation.33 | loop fusion | flops 8384512 | bytes 8404992 | tf_op jit(solution)/shard_map/reduce_sum | solution.py:10
  118.6 6.0 %multiply_convert_fusion.1 = bf16[256,4096]{1,0:T(8,128)(2,1)S(1)} fusion(bf16[256,1024]{1,0:T(8,128)(2,1)S(1)} %fusion.49, bf16[1024,4096]{1,0:T(8,128)(2,1)} %param.12), kind=kOutput, calls=%fused_computation.34 | convolution fusion | flops 2152726528 | bytes 11010048 | tf_op jit(solution)/shard_map/dot_general | solution.py:17
  124.7 1.4 copy-done.6
  126.1 1.2 fusion.73
  127.3 2.1 copy.60
  129.7 2.1 copy.59
  132.0 0.4 fusion.37
  132.4 8.5 %multiply_convert_fusion = bf16[512,4096]{1,0:T(8,128)(2,1)S(1)} fusion(bf16[1024,4096]{1,0:T(8,128)(2,1)} %param.12, bf16[512,1024]{1,0:T(8,128)(2,1)S(1)} %copy-done.3, f32[512]{0:T(512)S(1)} %add_rsqrt_fusion.1, f32[512]{0:T(512)S(1)} %broadcast_multiply_fusion.1), kind=kOutput, calls=%fused_computation.32 | convolution fusion | flops 4307550208 | bytes 13635584 | tf_op jit(solution)/shard_map/dot_general | solution.py:17
  141.0 1.9 convert_bitcast_fusion
  142.9 0.7 copy-done.2
  143.6 1.2 copy.85
  144.7 1.9 multiply_bitcast_fusion
  146.7 1.8 copy.76
  148.5 2.3 reduce_sum.109
  150.8 0.6 fusion.74
  151.6 1.2 compare_select_fusion.1
  153.2 0.9 copy.86
  154.1 49.5 %all-gather.5.cloned.1.call-done = bf16[2,1024,1024]{1,2,0:T(8,128)(2,1)} async-done(((bf16[2,128,1024]{1,2,0:T(8,128)(2,1)}), bf16[2,1024,1024]{1,2,0:T(8,128)(2,1)}) %all-gather.5.cloned.1.call-update) | async-done | bytes 4194320 | tf_op jit(solution)/shard_map/all_gather | solution.py:70
  203.5 73.8 %all-gather.3.cloned.1.call-done = bf16[2,1024,1024]{1,2,0:T(8,128)(2,1)} async-done(((bf16[2,128,1024]{1,2,0:T(8,128)(2,1)}), bf16[2,1024,1024]{1,2,0:T(8,128)(2,1)}) %all-gather.3.cloned.1.call-update) | async-done | bytes 4194320 | tf_op jit(solution)/shard_map/all_gather | solution.py:58
  277.4 70.4 %while.13 = (s32[]{:T(128)}, f32[8,2,128,128]{3,2,1,0:T(8,128)}, f32[8,512,128]{2,1,0:T(8,128)}, bf16[8,2,128,128]{3,2,1,0:T(8,128)(2,1)}, bf16[8,2,1024,128]{2,...) while((s32[]{:T(128)}, f32[8,2,128,128]{3,2,1,0:T(8,128)}, ...), condition=%wide.region_7.8_spmd.clone, body=%wide.region_6.7_spmd.clone.sunk | while | flops 682622976 | bytes 7029889 | solution.py:89
  277.4 1.3 constant_dynamic-slice_fusion.6
  278.6 1.0 copy.89
  279.9 3.7 fusion.98
  283.6 2.6 fusion.97
  286.2 1.3 constant_dynamic-slice_fusion.6
  287.4 1.0 copy.89
  288.7 3.7 fusion.98
  292.4 2.6 fusion.97
  295.0 1.3 constant_dynamic-slice_fusion.6
  296.2 1.0 copy.89
  297.3 0.3 copy.90
  297.5 3.7 %fusion.98 = f32[8,512,128]{2,1,0:T(8,128)} fusion(f32[8,512,128]{2,1,0:T(8,128)} %get-tuple-element.275, s32[]{:T(128)} %get-tuple-element.273, bf16[2048,128]{1,0:T(8,128)(2,1)} %bitcast.140, bf16[2048,128]{1,0:T(8,128)(2,1)S(1)} %bitcast.141, s32[2048]{0:T(1024)S(1)} %get-tuple-element.295, s32[512]{0:T(512)S(1)} %get-tuple-element.296, ...), kind=kOutput, calls=%fused_computation.6.clone.1 | convolution fusion | flops 546308096 | bytes 1455104 | tf_op jit(solution)/shard_map/while/body/eval_jaxpr/dot_general | solution.py:86
  301.2 2.6 fusion.97
  303.8 1.3 constant_dynamic-slice_fusion.6
  305.0 1.0 copy.89
  306.3 3.7 %fusion.98 = f32[8,512,128]{2,1,0:T(8,128)} fusion(f32[8,512,128]{2,1,0:T(8,128)} %get-tuple-element.275, s32[]{:T(128)} %get-tuple-element.273, bf16[2048,128]{1,0:T(8,128)(2,1)} %bitcast.140, bf16[2048,128]{1,0:T(8,128)(2,1)S(1)} %bitcast.141, s32[2048]{0:T(1024)S(1)} %get-tuple-element.295, s32[512]{0:T(512)S(1)} %get-tuple-element.296, ...), kind=kOutput, calls=%fused_computation.6.clone.1 | convolution fusion | flops 546308096 | bytes 1455104 | tf_op jit(solution)/shard_map/while/body/eval_jaxpr/dot_general | solution.py:86
  310.0 2.6 fusion.97
  312.6 1.3 constant_dynamic-slice_fusion.6
  313.8 1.0 copy.89
  314.9 0.3 copy.90
  315.1 3.7 %fusion.98 = f32[8,512,128]{2,1,0:T(8,128)} fusion(f32[8,512,128]{2,1,0:T(8,128)} %get-tuple-element.275, s32[]{:T(128)} %get-tuple-element.273, bf16[2048,128]{1,0:T(8,128)(2,1)} %bitcast.140, bf16[2048,128]{1,0:T(8,128)(2,1)S(1)} %bitcast.141, s32[2048]{0:T(1024)S(1)} %get-tuple-element.295, s32[512]{0:T(512)S(1)} %get-tuple-element.296, ...), kind=kOutput, calls=%fused_computation.6.clone.1 | convolution fusion | flops 546308096 | bytes 1455104 | tf_op jit(solution)/shard_map/while/body/eval_jaxpr/dot_general | solution.py:86
  318.8 2.6 fusion.97
  321.4 1.3 constant_dynamic-slice_fusion.6
  322.6 1.0 copy.89
  323.9 3.7 %fusion.98 = f32[8,512,128]{2,1,0:T(8,128)} fusion(f32[8,512,128]{2,1,0:T(8,128)} %get-tuple-element.275, s32[]{:T(128)} %get-tuple-element.273, bf16[2048,128]{1,0:T(8,128)(2,1)} %bitcast.140, bf16[2048,128]{1,0:T(8,128)(2,1)S(1)} %bitcast.141, s32[2048]{0:T(1024)S(1)} %get-tuple-element.295, s32[512]{0:T(512)S(1)} %get-tuple-element.296, ...), kind=kOutput, calls=%fused_computation.6.clone.1 | convolution fusion | flops 546308096 | bytes 1455104 | tf_op jit(solution)/shard_map/while/body/eval_jaxpr/dot_general | solution.py:86
  327.6 2.6 fusion.97
  330.2 1.3 constant_dynamic-slice_fusion.6
  331.5 1.0 copy.89
  332.5 0.3 copy.90
  332.8 3.7 %fusion.98 = f32[8,512,128]{2,1,0:T(8,128)} fusion(f32[8,512,128]{2,1,0:T(8,128)} %get-tuple-element.275, s32[]{:T(128)} %get-tuple-element.273, bf16[2048,128]{1,0:T(8,128)(2,1)} %bitcast.140, bf16[2048,128]{1,0:T(8,128)(2,1)S(1)} %bitcast.141, s32[2048]{0:T(1024)S(1)} %get-tuple-element.295, s32[512]{0:T(512)S(1)} %get-tuple-element.296, ...), kind=kOutput, calls=%fused_computation.6.clone.1 | convolution fusion | flops 546308096 | bytes 1455104 | tf_op jit(solution)/shard_map/while/body/eval_jaxpr/dot_general | solution.py:86
  336.4 2.6 fusion.97
  339.0 1.3 constant_dynamic-slice_fusion.6
  340.3 1.0 copy.89
  341.6 3.7 %fusion.98 = f32[8,512,128]{2,1,0:T(8,128)} fusion(f32[8,512,128]{2,1,0:T(8,128)} %get-tuple-element.275, s32[]{:T(128)} %get-tuple-element.273, bf16[2048,128]{1,0:T(8,128)(2,1)} %bitcast.140, bf16[2048,128]{1,0:T(8,128)(2,1)S(1)} %bitcast.141, s32[2048]{0:T(1024)S(1)} %get-tuple-element.295, s32[512]{0:T(512)S(1)} %get-tuple-element.296, ...), kind=kOutput, calls=%fused_computation.6.clone.1 | convolution fusion | flops 546308096 | bytes 1455104 | tf_op jit(solution)/shard_map/while/body/eval_jaxpr/dot_general | solution.py:86
  345.2 2.6 fusion.97
  347.8 2.6 fusion.71
  350.4 0.3 multiply_reduce_fusion
  350.8 0.8 copy-done.1
  352.0 0.6 copy.64
  352.9 3.7 add_convert_fusion
  356.5 1.8 convolution_add_fusion
  358.4 1.0 select_convert_fusion.2
  (54 shorter events, 3.5 us)
Async XLA Ops:
  7.2 345.5 %copy-start = (bf16[1024,1024]{1,0:T(8,128)(2,1)S(1)}, bf16[1024,1024]{1,0:T(8,128)(2,1)}, u32[]{:S(2)}) copy-start(bf16[1024,1024]{1,0:T(8,128)(2,1)} %param.13) | copy-start | bytes 6291460
  7.2 196.4 %all-gather.5.cloned.1.call-start = ((), (), s32[]{:S(2)}) async-start(), calls=%async_computation.2 | async-start | bytes 4718592 | tf_op jit(solution)/shard_map/all_gather | solution.py:70
  118.6 6.1 %copy-start.7 = (bf16[256,1024]{1,0:T(8,128)(2,1)}, bf16[256,1024]{1,0:T(8,128)(2,1)S(1)}, u32[]{:S(2)}) copy-start(bf16[256,1024]{1,0:T(8,128)(2,1)S(1)} %fusion.49) | copy-start | bytes 1572868
  124.7 1.4 copy-start.6
  127.3 4.5 %copy-start.3 = (bf16[512,1024]{1,0:T(8,128)(2,1)S(1)}, bf16[512,1024]{1,0:T(8,128)(2,1)}, u32[]{:S(2)}) copy-start(bf16[512,1024]{1,0:T(8,128)(2,1)} %param.9) | copy-start | bytes 3145732
  129.4 148.0 %all-gather.3.cloned.1.call-start = ((), (), s32[]{:S(2)}) async-start(), calls=%async_computation.1 | async-start | bytes 4718592 | tf_op jit(solution)/shard_map/all_gather | solution.py:58
  141.0 2.6 copy-start.2
  148.4 2.4 copy-start.9
  148.4 3.1 copy-start.10
  148.4 4.6 %copy-start.5 = (bf16[32,8,8,128]{3,1,2,0:T(8,128)(2,1)S(1)}, bf16[32,8,8,128]{3,1,2,0:T(8,128)(2,1)}, u32[]{:S(2)}) copy-start(bf16[32,8,8,128]{3,1,2,0:T(8,128)(2,1)} %get-tuple-element.176) | copy-start | bytes 1572868
  350.4 1.2 copy-start.1
  351.6 1.2 copy-start.4
  352.9 3.7 %copy-start.8 = (bf16[256,1024]{1,0:T(8,128)(2,1)S(1)}, bf16[256,1024]{1,0:T(8,128)(2,1)}, u32[]{:S(2)}) copy-start(bf16[256,1024]{1,0:T(8,128)(2,1)} %copy-done.7) | copy-start | bytes 1572868
Sparse Core Ops, SparseCore 0:
  129.5 73.9 all-gather.4
  205.7 71.6 all-gather.2
where the time goes:
time: 368 us; the launch traced here: 366 us
  waiting for transfers between devices  123 us (33%)
  blocking collectives  101 us (27%)
  matrix products  69.9 us (19%)
  local copies, waits for them, and re-layouts  34.3 us (9%)
  other arithmetic  23.2 us (6%)
  between operations  14.3 us (4%)
    all_to_all x1, blocking collectives, local(): lax.all_to_all(pooled, 'user', split_axis=1, concat_axis=0, tiled=True)  101 us
    all_gather x1, waiting for transfers between devices, local(): lax.all_gather(k_hist.reshape(users_dev, slots, width), 'cand', axis=1, t...  73.8 us
    all_gather x1, waiting for transfers between devices, local(): lax.all_gather(v_hist.reshape(users_dev, slots, width), 'cand', axis=1, t...  49.5 us
    dot_general x8, matrix products, one_head(): jnp.dot(weights_c, value_flat, preferred_element_type=jnp.float32)  29.4 us
    dynamic_slice x24, local copies, waits for them, and re-layouts, local(): lax.map(one_head, (qh_heads, qc_heads, k_heads, v_heads))  20.5 us
    dot_general x8, matrix products, one_head(): jnp.einsum('uqk,ukd->uqd', weights, value_h, preferred_element_type=jnp.f...  20.5 us
    dot_general x2, matrix products, project(): proj = jax.nn.silu(jnp.dot(feats, w_in, preferred_element_type=jnp.float32))  14.6 us
    reduce_sum x5, other arithmetic, layer_norm(): mean = jnp.mean(rows, axis=-1, keepdims=True)  7.53 us
  transfers between devices with their start and end apart: 2, of which 2 were waited for; matrix products, arithmetic and copies ran while one was open for 6% of the time, Pallas kernels for 0%

commit v1 on v0

v1 whole, which is shorter than its diff:
```python
import functools

import jax
import jax.numpy as jnp
from jax import lax
from jax.experimental import pallas as pl
from jax.experimental.pallas import tpu as pltpu
from jax.sharding import PartitionSpec as P

F32 = jnp.float32
BF16 = jnp.bfloat16
HEADS = 8
HD = 128
D = 1024
SLOTS = 128
ROWS = 512
NX, NZ = 4, 4
BLK = 128
WIDE = 256
STEPS = D // WIDE
HALF_SCALE = 0.5 / (HD**0.5)
VMEM = 56 * 1024 * 1024


def silu(v):
    half = v * 0.5
    return half + half * jnp.tanh(half)


def layer_norm(rows):
    mean = jnp.mean(rows, axis=-1, keepdims=True)
    centered = rows - mean
    var = jnp.mean(centered * centered, axis=-1, keepdims=True)
    return centered * lax.rsqrt(var + 1e-05)


def mm(a, b):
    return jnp.dot(a, b, preferred_element_type=F32)


def weights_of(queries, keys):
    s = lax.dot_general(queries, keys, (((1,), (1,)), ((), ())), preferred_element_type=F32)
    half = s * HALF_SCALE
    return half + half * jnp.tanh(half)


def cand_kernel(owner_ref, feats_ref, w_ref, xs_ref, u_ref, q_ref, a_ref, v_scr):
    step = pl.program_id(0)

    @pl.when(step == 0)
    def _():
        second = owner_ref[...].astype(F32)
        r_from = lax.broadcasted_iota(jnp.int32, (ROWS, ROWS), 0)
        r_to = lax.broadcasted_iota(jnp.int32, (ROWS, ROWS), 1)
        upper = jnp.where(r_from <= r_to, 1.0, 0.0).astype(BF16)
        ones_before = mm(jnp.broadcast_to(second, (8, ROWS)).astype(BF16), upper)[:1]
        index = lax.broadcasted_iota(jnp.int32, (1, ROWS), 1).astype(F32)
        n_first = ROWS - jnp.sum(second, axis=1, keepdims=True)
        place = jnp.where(second > 0.5, n_first + ones_before - 1.0, index - ones_before)
        onehot = jnp.where(r_from == place.astype(jnp.int32), 1.0, 0.0).astype(BF16)
        x = layer_norm(feats_ref[...].astype(F32)).astype(BF16)
        xs_ref[...] = mm(onehot, x).astype(BF16)

    proj = silu(mm(xs_ref[...], w_ref[...])).astype(BF16)

    @pl.when(step == 0)
    def _():
        u_ref[...] = proj

    @pl.when(step == 1)
    def _():
        v_scr[...] = proj

    @pl.when(step == 2)
    def _():
        q_ref[...] = proj

    @pl.when(step == 3)
    def _():
        prod = q_ref[...].astype(F32) * proj.astype(F32)
        for h in range(HEADS):
            cols = slice(h * HD, (h + 1) * HD)
            half = jnp.sum(prod[:, cols], axis=-1, keepdims=True) * HALF_SCALE
            own = (half + half * jnp.tanh(half)).astype(BF16).astype(F32)
            a_ref[:, cols] = own * v_scr[:, cols].astype(F32)


def cand_project(owner_row, feats, w_in):
    whole = lambda i: (0, 0)
    return pl.pallas_call(
        cand_kernel,
        grid=(4,),
        in_specs=[
            pl.BlockSpec((1, ROWS), whole),
            pl.BlockSpec((ROWS, D), whole),
            pl.BlockSpec((D, D), lambda i: (0, i)),
        ],
        out_specs=[pl.BlockSpec((ROWS, D), whole)] * 4,
        out_shape=[
            jax.ShapeDtypeStruct((ROWS, D), BF16),
            jax.ShapeDtypeStruct((ROWS, D), BF16),
            jax.ShapeDtypeStruct((ROWS, D), BF16),
            jax.ShapeDtypeStruct((ROWS, D), F32),
        ],
        scratch_shapes=[pltpu.VMEM((ROWS, D), BF16)],
        compiler_params=pltpu.CompilerParams(vmem_limit_bytes=VMEM),
        cost_estimate=pl.CostEstimate(
            flops=2 * ROWS * D * 4 * D, bytes_accessed=16 << 20, transcendentals=ROWS * 4 * D
        ),
        name="cand_project",
    )(owner_row, feats, w_in)


def attend_kernel(last, scal_ref, *refs):
    x_refs = refs[:4]
    wu_ref, wv_ref, wq_ref, wk_ref, wo_ref, q_ref, a_in_ref = refs[4:11]
    refs = refs[11:]
    if last:
        u_ref, xs_ref, owner_ref, hist_ref, out_ref, k_scr, v_scr, u_scr, ah_scr, a_ref = refs
    else:
        hist_ref, a_ref, k_scr, v_scr, u_scr, ah_scr = refs
    step = pl.program_id(0)
    length = scal_ref[0]
    row_lo = scal_ref[1]
    row_hi = scal_ref[2]
    my_off = scal_ref[3]
    cols = pl.ds(pl.multiple_of(step * WIDE, WIDE), WIDE)
    x_own = x_refs[0][0]
    row_iota = lax.broadcasted_iota(jnp.int32, (SLOTS, 1), 0)

    @pl.when(step == 0)
    def _():
        a_ref[...] = a_in_ref[...]

    for p in range(4):
        x = x_refs[p][...].reshape(2 * SLOTS, D)
        rows = slice(p * 2 * SLOTS, (p + 1) * 2 * SLOTS)
        k_scr[rows, :] = silu(mm(x, wk_ref[...])).astype(BF16)
        v = silu(mm(x, wv_ref[...])).astype(BF16)
        for e in range(2):
            piece = v[e * SLOTS : (e + 1) * SLOTS]
            off = scal_ref[4 + 2 * p + e]
            at = (2 * p + e) * SLOTS
            v_scr[at : at + SLOTS, :] = jnp.where(row_iota < length - off, piece, jnp.zeros_like(piece))

    u_scr[:, cols] = silu(mm(x_own, wu_ref[...])).astype(BF16)
    q_hist = silu(mm(x_own, wq_ref[...])).astype(BF16)
    ahead = lax.broadcasted_iota(jnp.int32, (SLOTS, SLOTS), 0) - lax.broadcasted_iota(
        jnp.int32, (SLOTS, SLOTS), 1
    )
    for h in range(WIDE // HD):
        hc = slice(h * HD, (h + 1) * HD)
        w = weights_of(q_hist[:, hc], k_scr[:, hc])
        parts = []
        for n in range(8):
            seen = ahead >= scal_ref[4 + n] - my_off
            parts.append(jnp.where(seen, w[:, n * SLOTS : (n + 1) * SLOTS], 0.0).astype(BF16))
        out_cols = pl.ds(pl.multiple_of(step * WIDE + h * HD, HD), HD)
        ah_scr[:, out_cols] = mm(jnp.concatenate(parts, axis=1), v_scr[:, hc])

    first_block = row_lo // BLK
    end_block = (row_hi + BLK - 1) // BLK

    @pl.loop(first_block, end_block)
    def _(blk):
        start = pl.multiple_of(blk * BLK, BLK)
        rows = pl.ds(start, BLK)
        index = start + lax.broadcasted_iota(jnp.int32, (BLK, 1), 0)
        mine = (index >= row_lo) & (index < row_hi)
        for h in range(WIDE // HD):
            hc = slice(h * HD, (h + 1) * HD)
            out_cols = pl.ds(pl.multiple_of(step * WIDE + h * HD, HD), HD)
            w = weights_of(q_ref[rows, out_cols], k_scr[:, hc]).astype(BF16)
            part = mm(w, v_scr[:, hc])
            a_ref[rows, out_cols] += jnp.where(mine, part, 0.0)

    @pl.when(step == STEPS - 1)
    def _():
        y = (layer_norm(ah_scr[...]) * u_scr[...].astype(F32)).astype(BF16)
        res = mm(y, wo_ref[...]) + x_own.astype(F32)
        hist_ref[...] = jnp.where(my_off + row_iota < length, res, 0.0).astype(BF16)
        if last:
            yc = (layer_norm(a_ref[...]) * u_ref[...].astype(F32)).astype(BF16)
            done = (mm(yc, wo_ref[...]) + xs_ref[...].astype(F32)).astype(BF16)
            r_row = lax.broadcasted_iota(jnp.int32, (ROWS, ROWS), 0)
            r_col = lax.broadcasted_iota(jnp.int32, (ROWS, ROWS), 1)
            second = owner_ref[...].astype(F32)
            lower = jnp.where(r_col <= r_row, 1.0, 0.0).astype(BF16)
            ones_before = mm(lower, jnp.broadcast_to(second, (ROWS, HD)).astype(BF16))[:, :1]
            index = lax.broadcasted_iota(jnp.int32, (ROWS, 1), 0).astype(F32)
            n_first = ROWS - jnp.sum(second, axis=0, keepdims=True)
            place = jnp.where(second > 0.5, n_first + ones_before - 1.0, index - ones_before)
            back = jnp.where(r_col == place.astype(jnp.int32), 1.0, 0.0).astype(BF16)
            out_ref[...] = mm(back, done).astype(BF16)


def attend(last, scal, pieces, w_in, w_out, q_cand, a_cand, extra):
    whole = lambda i, s: (0, 0)
    part = lambda n: pl.BlockSpec((D, WIDE), lambda i, s: (0, n * STEPS + i))
    rows_spec = pl.BlockSpec((ROWS, D), whole)
    in_specs = [pl.BlockSpec((2, SLOTS, D), lambda i, s: (0, 0, 0))] * 4
    in_specs += [part(0), part(1), part(2), part(3), pl.BlockSpec((D, D), whole)]
    in_specs += [rows_spec, rows_spec]
    hist_spec = pl.BlockSpec((SLOTS, D), whole)
    hist_shape = jax.ShapeDtypeStruct((SLOTS, D), BF16)
    scratch = [
        pltpu.VMEM((8 * SLOTS, WIDE), BF16),
        pltpu.VMEM((8 * SLOTS, WIDE), BF16),
        pltpu.VMEM((SLOTS, D), BF16),
        pltpu.VMEM((SLOTS, D), F32),
    ]
    if last:
        in_specs += [rows_spec, rows_spec, pl.BlockSpec((ROWS, 1), whole)]
        out_specs = [hist_spec, rows_spec]
        out_shape = [hist_shape, jax.ShapeDtypeStruct((ROWS, D), BF16)]
        scratch.append(pltpu.VMEM((ROWS, D), F32))
    else:
        out_specs = [hist_spec, rows_spec]
        out_shape = [hist_shape, jax.ShapeDtypeStruct((ROWS, D), F32)]
    return pl.pallas_call(
        functools.partial(attend_kernel, last),
        grid_spec=pltpu.PrefetchScalarGridSpec(
            num_scalar_prefetch=1,
            grid=(STEPS,),
            in_specs=in_specs,
            out_specs=out_specs,
            scratch_shapes=scratch,
        ),
        out_shape=out_shape,
        compiler_params=pltpu.CompilerParams(vmem_limit_bytes=VMEM),
        cost_estimate=pl.CostEstimate(
            flops=12 * 10**9, bytes_accessed=24 << 20, transcendentals=4 * 10**6
        ),
        name="attend_last" if last else "attend_first",
    )(scal, *pieces, w_in, w_in, w_in, w_in, w_out, q_cand, a_cand, *extra)


def user_at(x, y, core):
    return (x * 2 + y) * 2 + core


def user_perm(dx, dy, dcore):
    pairs = []
    for u in range(4 * NX):
        x, y, core = u >> 2, (u >> 1) & 1, u & 1
        pairs.append((u, user_at((x + dx) % NX, y ^ dy, core ^ dcore)))
    return pairs


def cand_perm(dz, dy):
    return [(c, (((c >> 1) + dz) % NZ) * 2 + ((c & 1) ^ dy)) for c in range(2 * NZ)]


def pick(array, at, axis):
    return lax.dynamic_index_in_dim(array, at, axis, keepdims=False)


def reduce_tables(view, x, y, core):
    with jax.named_scope("sum_core"):
        got = lax.ppermute(pick(view, 1 - core, 2), "user", user_perm(0, 0, 1))
        mine = pick(view, core, 2)
        toward = []
        for d in range(NX):
            to = lax.rem(x + d, NX)
            pair = pick(mine, to, 0).astype(F32) + pick(got, to, 0).astype(F32)
            toward.append(pair.astype(BF16))
    with jax.named_scope("sum_x"):
        arrived = [lax.ppermute(toward[d], "user", user_perm(d, 0, 0)) for d in (1, 3, 2)]
        total = toward[0].astype(F32)
        for got in arrived:
            total = total + got.astype(F32)
    with jax.named_scope("sum_y"):
        other = lax.ppermute(pick(total, 1 - y, 0).astype(BF16), "user", user_perm(0, 1, 0))
        return pick(total, y, 0) + other.astype(F32)


def local(pooled, cand_feats, hist_len, cand_user, w_in, w_out):
    user = lax.axis_index("user")
    cand = lax.axis_index("cand")
    x, y, core = user >> 2, (user >> 1) & 1, user & 1
    z, y_hi = cand >> 1, cand & 1
    owner = cand_user - 2 * user
    n_first = ROWS - jnp.sum(owner)
    xs, u_cand, q_cand, a_cand = cand_project(owner.reshape(1, ROWS), cand_feats, w_in)
    view = pooled.reshape(NX, 2, 2, 2, SLOTS, D)
    offsets = []
    for dz in (0, -1, 1, 2):
        for e in range(2):
            offsets.append(SLOTS * (((z + dz + NZ) % NZ) * 2 + (y_hi ^ e)))
    gathered = []
    for j in range(2):
        emb = reduce_tables(view[:, :, :, j], x, y, core)
        with jax.named_scope("gather"):
            own = layer_norm(emb).astype(BF16)
            near = lax.ppermute(own, "cand", cand_perm(0, 1))
            pair = jnp.stack([own, near])
            gathered.append(
                [pair] + [lax.ppermute(pair, "cand", cand_perm(dz, 0)) for dz in (1, -1, 2)]
            )
    outs = []
    for j in range(2):
        last = j == 1
        rows = [n_first, jnp.int32(ROWS)] if last else [jnp.int32(0), n_first]
        scal = jnp.stack([hist_len[j]] + rows + [cand * SLOTS] + offsets).astype(jnp.int32)
        extra = (u_cand, xs, owner.reshape(ROWS, 1)) if last else ()
        out, a_cand = attend(last, scal, gathered[j], w_in, w_out, q_cand, a_cand, extra)
        outs.append(out)
    return jnp.stack(outs), a_cand


def solution(mesh):
    placed = (
        P("user", None, "cand", None),
        P(("user", "cand"), None),
        P("user"),
        P(("user", "cand")),
        P(),
        P(),
    )
    return jax.shard_map(
        local,
        mesh=mesh,
        in_specs=placed,
        out_specs=(P("user", "cand", None), P(("user", "cand"), None)),
        check_vma=False,
    )
```

time: 368 us -> 169 us (0.46)
  blocking collectives: 101 us -> 0 us
  waiting for transfers between devices: 123 us -> 35.5 us
  matrix products: 69.9 us -> 0 us
  Pallas kernels: 0 us -> 60 us
  starting transfers between devices: 0.26 us -> 40.9 us
  local copies, waits for them, and re-layouts: 34.3 us -> 17.2 us
  between operations: 14.3 us -> 1.38 us
  other arithmetic: 23.2 us -> 13.8 us
    all_gather x2 -> x0, waiting for transfers between devices: 123 us -> none  [the longest x1 73.8 us: local(): lax.all_gather(k_hist.reshape(users_dev, slots, width), 'cand', axis=1, t...]
    all_to_all x1 -> x0, blocking collectives: 101 us -> none  [local(): lax.all_to_all(pooled, 'user', split_axis=1, concat_axis=0, tiled=True)]
    dot_general x20 -> x0, matrix products: 69.9 us -> none  [the longest x8 29.4 us: one_head(): jnp.dot(weights_c, value_flat, preferred_element_type=jnp.float32)]
    pallas_call x0 -> x3, Pallas kernels: none -> 60 us  [the longest x2 47.6 us: attend(): pl.pallas_call(functools.partial(attend_kernel, last), grid_spec=pltpu.Pr...]
    ppermute x0 -> x18, starting transfers between devices: none -> 40.9 us  [the longest x6 20.9 us: reduce_tables(): lax.ppermute(toward[d], 'user', user_perm(d, 0, 0))]
    ppermute x0 -> x18, waiting for transfers between devices: none -> 35.5 us  [the longest x6 17.1 us: reduce_tables(): lax.ppermute(toward[d], 'user', user_perm(d, 0, 0))]
    dynamic_slice x24 -> x0, local copies, waits for them, and re-layouts: 20.5 us -> none  [local(): lax.map(one_head, (qh_heads, qc_heads, k_heads, v_heads))]
    reduce_sum x5 -> x2, other arithmetic: 7.53 us -> 0.27 us  [layer_norm(): mean = jnp.mean(rows, axis=-1, keepdims=True)]
  transfers between devices with their start and end apart: 2 -> 18, of which waited for: 2 -> 7; matrix products, arithmetic and copies ran while one was open for 6% -> 11% of each run, Pallas kernels for 0% -> 21%
where the time goes in v1:
time: 169 us
  Pallas kernels  60 us (36%)
  starting transfers between devices  40.9 us (24%)
  waiting for transfers between devices  35.5 us (21%)
  local copies, waits for them, and re-layouts  17.2 us (10%)
  other arithmetic  13.8 us (8%)
    pallas_call x2, Pallas kernels, attend(): pl.pallas_call(functools.partial(attend_kernel, last), grid_spec=pltpu.Pr...  47.6 us
    ppermute x6, starting transfers between devices, reduce_tables(): lax.ppermute(toward[d], 'user', user_perm(d, 0, 0))  20.9 us
    ppermute x6, waiting for transfers between devices, reduce_tables(): lax.ppermute(toward[d], 'user', user_perm(d, 0, 0))  17.1 us
    pallas_call x1, Pallas kernels, cand_project(): pl.pallas_call(cand_kernel, grid=(4,), in_specs=[pl.BlockSpec((1, ROWS),...  12.4 us
    ppermute x6, starting transfers between devices, local(): lax.ppermute(pair, 'cand', cand_perm(dz, 0))  9.85 us
    ppermute x6, waiting for transfers between devices, local(): lax.ppermute(pair, 'cand', cand_perm(dz, 0))  7.39 us
    convert_element_type x2, other arithmetic, reduce_tables(): toward.append(pair.astype(BF16))  6.28 us
    ppermute x2, starting transfers between devices, local(): near = lax.ppermute(own, 'cand', cand_perm(0, 1))  6.25 us
  transfers between devices with their start and end apart: 18, of which 7 were waited for; matrix products, arithmetic and copies ran while one was open for 11% of the time, Pallas kernels for 21%

profile of v1, /device:TPU:0, one launch (start us, length us, event | category | flops | bytes accessed | tf_op | source)
XLA Modules:
  0.0 168.7 jit_solution(12158853697340004076)
XLA Ops:
  0.6 6.1 %fusion.13 = (bf16[4,2,2,1,128,1024]{5,4,3,2,1,0:T(8,128)(2,1)}, bf16[4,2,2,1,128,1024]{5,4,3,2,1,0:T(8,128)(2,1)}) fusion(bf16[4,2,2,2,128,1024]{5,4,3,2,1,0:T(8,128)(2,1)} %bitcast.111), kind=kLoop, calls=%fused_computation.41 | loop fusion | bytes 16777216 | tf_op jit(solution)/shard_map/slice | solution.py:292
  6.8 3.2 %dynamic-slice_bitcast_fusion.1 = bf16[4,2,128,1024]{3,2,1,0:T(8,128)(2,1)} fusion(bf16[4,2,2,1,128,1024]{5,4,3,2,1,0:T(8,128)(2,1)} %get-tuple-element.20, s32[]{:T(128)S(6)} %select_n.88), kind=kLoop, calls=%fused_computation.1 | loop fusion | bytes 4194308 | tf_op jit(solution)/shard_map/sum_core/jit(dynamic_index_in_dim)/squeeze | solution.py:255
  10.0 0.0 collective-permute-start
  10.0 1.5 dynamic-slice_bitcast_fusion
  11.5 0.5 collective-permute-start.9
  12.0 2.5 %collective-permute-done = bf16[4,2,128,1024]{3,2,1,0:T(8,128)(2,1)} collective-permute-done((bf16[4,2,128,1024]{3,2,1,0:T(8,128)(2,1)}, bf16[4,2,128,1024]{3,2,1,0:T(8,128)(2,1)}, u32[]{:S(2)}, u32[]{:S(2)}) %collective-permute-start) | collective-permute-done | bytes 2097184 | tf_op jit(solution)/shard_map/sum_core/ppermute | solution.py:260
  14.5 3.4 %fusion.6 = (bf16[2,128,1024]{2,1,0:T(8,128)(2,1)}, bf16[2,128,1024]{2,1,0:T(8,128)(2,1)S(1)}, bf16[2,128,1024]{2,1,0:T(8,128)(2,1)S(1)}) fusion(bf16[4,2,128,1024]{3,2,1,0:T(8,128)(2,1)} %collective-permute-done, s32[]{:T(128)S(6)} %select_n.89, bf16[4,2,2,1,128,1024]{5,4,3,2,1,0:T(8,128)(2,1)} %get-tuple-element.20, s32[]{:T(128)S(6)} %select_n.90, ...), kind=kLoop, calls=%fused_computation.15 | loop fusion | flops 3145728 | bytes 4718620 | tf_op jit(solution)/shard_map/sum_core/convert_element_type | solution.py:266
  17.9 1.6 collective-permute-start.1
  19.4 1.7 collective-permute-start.2
  21.1 1.9 %collective-permute-start.3 = (bf16[2,128,1024]{2,1,0:T(8,128)(2,1)S(1)}, bf16[2,128,1024]{2,1,0:T(8,128)(2,1)}, u32[]{:S(2)}, u32[]{:S(2)}) collective-permute-start(bf16[2,128,1024]{2,1,0:T(8,128)(2,1)S(1)} %get-tuple-element.23), channel_id=1, source_target_pairs={{0,64},{8,72},{16,80},{24,88},{32,96},{40,104},{48,112},{56,120},{... | collective-permute-start | bytes 1572872 | tf_op jit(solution)/shard_map/sum_x/ppermute | solution.py:268
  23.0 0.6 fusion.12
  23.6 0.0 collective-permute-done.9
  23.6 2.9 %fusion.2 = (bf16[2,128,1024]{2,1,0:T(8,128)(2,1)}, bf16[2,128,1024]{2,1,0:T(8,128)(2,1)}, bf16[2,128,1024]{2,1,0:T(8,128)(2,1)}) fusion(bf16[4,2,128,1024]{3,2,1,0:T(8,128)(2,1)S(1)} %collective-permute-done.9, s32[]{:T(128)S(6)} %select_n.89, bf16[4,2,2,1,128,1024]{5,4,3,2,1,0:T(8,128)(2,1)} %get-tuple-element.21, s32[]{:T(128)S(6)} %select_n.90, ...), kind=kLoop, calls=%fused_computation.7 | loop fusion | flops 3145728 | bytes 4718620 | tf_op jit(solution)/shard_map/sum_core/convert_element_type | solution.py:266
  26.6 0.6 collective-permute-start.10
  27.1 2.6 %collective-permute-start.11 = (bf16[2,128,1024]{2,1,0:T(8,128)(2,1)}, bf16[2,128,1024]{2,1,0:T(8,128)(2,1)}, u32[]{:S(2)}, u32[]{:S(2)}) collective-permute-start(bf16[2,128,1024]{2,1,0:T(8,128)(2,1)} %get-tuple-element.27), channel_id=1, source_target_pairs={{0,96},{8,104},{16,112},{24,120},{32,0},{40,8},{48,16},{56,24},{64... | collective-permute-start | bytes 1572872 | tf_op jit(solution)/shard_map/sum_x/ppermute | solution.py:268
  29.8 4.9 %collective-permute-done.1 = bf16[2,128,1024]{2,1,0:T(8,128)(2,1)} collective-permute-done((bf16[2,128,1024]{2,1,0:T(8,128)(2,1)}, bf16[2,128,1024]{2,1,0:T(8,128)(2,1)}, u32[]{:S(2)}, u32[]{:S(2)}) %collective-permute-start.1) | collective-permute-done | bytes 524320 | tf_op jit(solution)/shard_map/sum_x/ppermute | solution.py:268
  34.7 12.6 %collective-permute-start.12 = (bf16[2,128,1024]{2,1,0:T(8,128)(2,1)}, bf16[2,128,1024]{2,1,0:T(8,128)(2,1)}, u32[]{:S(2)}, u32[]{:S(2)}) collective-permute-start(bf16[2,128,1024]{2,1,0:T(8,128)(2,1)} %get-tuple-element.26), channel_id=1, source_target_pairs={{0,64},{8,72},{16,80},{24,88},{32,96},{40,104},{48,112},{56,120},{... | collective-permute-start | bytes 1572872 | tf_op jit(solution)/shard_map/sum_x/ppermute | solution.py:268
  47.3 0.8 copy.10.refs_13_
  48.7 0.7 fusion.14
  49.3 1.4 stack.83.scal_ref
  50.7 1.4 stack.88.scal_ref
  52.1 0.0 collective-permute-done.2
  52.1 0.0 collective-permute-done.3
  52.1 2.1 %convert_add_fusion.9 = f32[2,128,1024]{2,1,0:T(8,128)S(1)} fusion(bf16[2,128,1024]{2,1,0:T(8,128)(2,1)} %collective-permute-done.3, bf16[2,128,1024]{2,1,0:T(8,128)(2,1)} %collective-permute-done.2, bf16[2,128,1024]{2,1,0:T(8,128)(2,1)} %collective-permute-done.1, bf16[4,2,128,1024]{3,2,1,0:T(8,128)(2,1)} %collective-permute-done, s32[]{:T(128)S(6)} %select_n.84, ...), kind=kLoop, calls=%fused_computation.19 | loop fusion | flops 2883584 | bytes 3670028 | tf_op jit(solution)/shard_map/sum_x/add | solution.py:271
  54.3 1.7 collective-permute-start.4
  55.9 0.0 collective-permute-done.10
  55.9 0.9 collective-permute-done.11
  56.9 11.3 %collective-permute-done.12 = bf16[2,128,1024]{2,1,0:T(8,128)(2,1)} collective-permute-done((bf16[2,128,1024]{2,1,0:T(8,128)(2,1)}, bf16[2,128,1024]{2,1,0:T(8,128)(2,1)}, u32[]{:S(2)}, u32[]{:S(2)}) %collective-permute-start.12) | collective-permute-done | bytes 524320 | tf_op jit(solution)/shard_map/sum_x/ppermute | solution.py:268
  68.2 1.9 %convert_add_fusion.8 = f32[2,128,1024]{2,1,0:T(8,128)S(1)} fusion(bf16[2,128,1024]{2,1,0:T(8,128)(2,1)} %collective-permute-done.12, bf16[2,128,1024]{2,1,0:T(8,128)(2,1)} %collective-permute-done.11, bf16[2,128,1024]{2,1,0:T(8,128)(2,1)} %collective-permute-done.10, bf16[4,2,128,1024]{3,2,1,0:T(8,128)(2,1)S(1)} %collective-permute-done.9, ...), kind=kLoop, calls=%fused_computation.18 | loop fusion | flops 2883584 | bytes 3670028 | tf_op jit(solution)/shard_map/sum_x/add | solution.py:271
  70.2 1.7 collective-permute-start.13
  71.8 0.0 collective-permute-done.4
  71.8 0.1 fusion.10
  72.0 0.2 multiply_reduce_fusion.1
  72.2 0.1 multiply_convert_fusion.1
  72.3 3.0 %collective-permute-start.5 = (bf16[128,1024]{1,0:T(8,128)(2,1)S(1)}, bf16[128,1024]{1,0:T(8,128)(2,1)S(1)}, u32[]{:S(2)}, u32[]{:S(2)}) collective-permute-start(bf16[128,1024]{1,0:T(8,128)(2,1)S(1)} %multiply_convert_fusion.1), channel_id=1, source_target_pairs={{0,1},{1,0},{2,3},{3,2},{4,5},{5,4},{6,7},{7,6},{8,9},{9,8},{10,11... | collective-permute-start | bytes 786440 | tf_op jit(solution)/shard_map/gather/ppermute | solution.py:295
  75.3 4.2 %collective-permute-done.13 = bf16[128,1024]{1,0:T(8,128)(2,1)S(1)} collective-permute-done((bf16[128,1024]{1,0:T(8,128)(2,1)S(1)}, bf16[128,1024]{1,0:T(8,128)(2,1)S(1)}, u32[]{:S(2)}, u32[]{:S(2)}) %collective-permute-start.13) | collective-permute-done | bytes 262176 | tf_op jit(solution)/shard_map/sum_y/ppermute | solution.py:273
  79.5 0.1 fusion.11
  79.6 0.2 multiply_reduce_fusion
  79.8 0.1 multiply_convert_fusion
  80.0 3.3 %collective-permute-start.14 = (bf16[128,1024]{1,0:T(8,128)(2,1)S(1)}, bf16[128,1024]{1,0:T(8,128)(2,1)S(1)}, u32[]{:S(2)}, u32[]{:S(2)}) collective-permute-start(bf16[128,1024]{1,0:T(8,128)(2,1)S(1)} %multiply_convert_fusion), channel_id=1, source_target_pairs={{0,1},{1,0},{2,3},{3,2},{4,5},{5,4},{6,7},{7,6},{8,9},{9,8},{10,11... | collective-permute-start | bytes 786440 | tf_op jit(solution)/shard_map/gather/ppermute | solution.py:295
  83.3 4.3 %collective-permute-done.5 = bf16[128,1024]{1,0:T(8,128)(2,1)S(1)} collective-permute-done((bf16[128,1024]{1,0:T(8,128)(2,1)S(1)}, bf16[128,1024]{1,0:T(8,128)(2,1)S(1)}, u32[]{:S(2)}, u32[]{:S(2)}) %collective-permute-start.5) | collective-permute-done | bytes 262176 | tf_op jit(solution)/shard_map/gather/ppermute | solution.py:295
  87.6 0.1 pad_maximum_fusion.refs_0_
  87.6 0.0 copy-start.1
  87.6 2.0 %collective-permute-start.6 = (bf16[2,128,1024]{2,1,0:T(8,128)(2,1)S(1)}, bf16[2,128,1024]{2,1,0:T(8,128)(2,1)S(1)}, u32[]{:S(2)}, u32[]{:S(2)}) collective-permute-start(bf16[2,128,1024]{2,1,0:T(8,128)(2,1)S(1)} %pad_maximum_fusion.refs_0_), channel_id=1, source_target_pairs={{0,2},{1,3},{2,4},{3,5},{4,6},{5,7},{6,0},{7,1},{8,10},{9,11},{10,... | collective-permute-start | bytes 1572872 | tf_op jit(solution)/shard_map/gather/ppermute | solution.py:298
  89.6 2.2 %collective-permute-start.7 = (bf16[2,128,1024]{2,1,0:T(8,128)(2,1)S(1)}, bf16[2,128,1024]{2,1,0:T(8,128)(2,1)S(1)}, u32[]{:S(2)}, u32[]{:S(2)}) collective-permute-start(bf16[2,128,1024]{2,1,0:T(8,128)(2,1)S(1)} %pad_maximum_fusion.refs_0_), channel_id=1, source_target_pairs={{0,6},{1,7},{2,0},{3,1},{4,2},{5,3},{6,4},{7,5},{8,14},{9,15},{10,... | collective-permute-start | bytes 1572872 | tf_op jit(solution)/shard_map/gather/ppermute | solution.py:298
  91.8 1.8 %collective-permute-start.8 = (bf16[2,128,1024]{2,1,0:T(8,128)(2,1)S(1)}, bf16[2,128,1024]{2,1,0:T(8,128)(2,1)S(1)}, u32[]{:S(2)}, u32[]{:S(2)}) collective-permute-start(bf16[2,128,1024]{2,1,0:T(8,128)(2,1)S(1)} %pad_maximum_fusion.refs_0_), channel_id=1, source_target_pairs={{0,4},{1,5},{2,6},{3,7},{4,0},{5,1},{6,2},{7,3},{8,12},{9,13},{10,... | collective-permute-start | bytes 1572872 | tf_op jit(solution)/shard_map/gather/ppermute | solution.py:298
  93.6 12.4 %cand_project.1 = (bf16[512,1024]{1,0:T(8,128)(2,1)}, bf16[512,1024]{1,0:T(8,128)(2,1)}, bf16[512,1024]{1,0:T(8,128)(2,1)}, f32[512,1024]{1,0:T(8,128)}) custom-call(s32[1,512]{1,0:T(1,128)} %bitcast.119, bf16[512,1024]{1,0:T(8,128)(2,1)} %feats_ref.1, bf16[1024,4096]{1,0:T(8,128)(2,1)} %refs_7_.3), custom_call_target="tpu_custom_call" | custom-call | flops 4294967296 | bytes 16777216 | tf_op jit(solution)/shard_map/cand_project/pallas_call | solution.py:90
  106.0 0.0 collective-permute-done.14
  106.0 0.1 pad_maximum_fusion.1.refs_0_
  106.0 0.0 copy-start.2
  106.0 1.1 collective-permute-start.15
  107.1 2.2 %collective-permute-start.16 = (bf16[2,128,1024]{2,1,0:T(8,128)(2,1)S(1)}, bf16[2,128,1024]{2,1,0:T(8,128)(2,1)S(1)}, u32[]{:S(2)}, u32[]{:S(2)}) collective-permute-start(bf16[2,128,1024]{2,1,0:T(8,128)(2,1)S(1)} %pad_maximum_fusion.1.refs_0_), channel_id=1, source_target_pairs={{0,6},{1,7},{2,0},{3,1},{4,2},{5,3},{6,4},{7,5},{8,14},{9,15},{10,... | collective-permute-start | bytes 1572872 | tf_op jit(solution)/shard_map/gather/ppermute | solution.py:298
  109.3 0.0 collective-permute-done.6.refs_1_
  109.3 0.6 collective-permute-start.17
  109.9 0.0 collective-permute-done.7.refs_2_
  109.9 7.4 %collective-permute-done.8.refs_3_ = bf16[2,128,1024]{2,1,0:T(8,128)(2,1)S(1)} collective-permute-done((bf16[2,128,1024]{2,1,0:T(8,128)(2,1)S(1)}, bf16[2,128,1024]{2,1,0:T(8,128)(2,1)S(1)}, u32[]{:S(2)}, u32[]{:S(2)}) %collective-permute-start.8) | collective-permute-done | bytes 524320 | tf_op jit(solution)/shard_map/gather/ppermute | solution.py:298
  117.3 0.9 copy-done.11
  118.2 23.8 %attend_first.1 = (bf16[128,1024]{1,0:T(8,128)(2,1)}, f32[512,1024]{1,0:T(8,128)}) custom-call(s32[12]{0:T(128)} %stack.83.scal_ref, bf16[2,128,1024]{2,1,0:T(8,128)(2,1)} %copy-done.1, bf16[2,128,1024]{2,1,0:T(8,128)(2,1)} %copy-done.7, bf16[2,128,1024]{2,1,0:T(8,128)(2,1)} %copy-done.9, bf16[2,128,1024]{2,1,0:T(8,128)(2,1)} %copy-done.11, ...), custom_call_target="tpu_custom_call" | custom-call | flops 12000000000 | bytes 25165824 | tf_op jit(solution)/shard_map/attend_first/pallas_call | solution.py:220
  142.0 0.0 collective-permute-done.17.refs_3_
  142.0 0.7 copy-done.8
  142.8 0.2 copy-done.10
  143.0 0.2 copy-done.12
  143.1 23.8 %attend_last.1 = (bf16[128,1024]{1,0:T(8,128)(2,1)}, bf16[512,1024]{1,0:T(8,128)(2,1)}) custom-call(s32[12]{0:T(128)} %stack.88.scal_ref, bf16[2,128,1024]{2,1,0:T(8,128)(2,1)} %copy-done.2, bf16[2,128,1024]{2,1,0:T(8,128)(2,1)} %copy-done.8, bf16[2,128,1024]{2,1,0:T(8,128)(2,1)} %copy-done.10, bf16[2,128,1024]{2,1,0:T(8,128)(2,1)} %copy-done.12, ...), custom_call_target="tpu_custom_call" | custom-call | flops 12000000000 | bytes 25165824 | tf_op jit(solution)/shard_map/attend_last/pallas_call | solution.py:220
  166.9 1.8 %pad_maximum_fusion.2 = bf16[2,128,1024]{2,1,0:T(8,128)(2,1)} fusion(bf16[1,128,1024]{2,1,0:T(8,128)(2,1)} %bitcast.117, bf16[1,128,1024]{2,1,0:T(8,128)(2,1)S(1)} %bitcast.114), kind=kLoop, calls=%fused_computation.22 | loop fusion | flops 262144 | bytes 1048576 | tf_op jit(solution)/shard_map/stack | solution.py:308
  (28 shorter events, 0.2 us)
Async XLA Ops:
  6.8 3.2 %copy-start = (bf16[4,2,2,1,128,1024]{5,4,3,2,1,0:T(8,128)(2,1)S(1)}, bf16[4,2,2,1,128,1024]{5,4,3,2,1,0:T(8,128)(2,1)}, u32[]{:S(2)}) copy-start(bf16[4,2,2,1,128,1024]{5,4,3,2,1,0:T(8,128)(2,1)} %get-tuple-element.21) | copy-start | bytes 12582916
  10.0 4.5 %collective-permute-start = (bf16[4,2,128,1024]{3,2,1,0:T(8,128)(2,1)}, bf16[4,2,128,1024]{3,2,1,0:T(8,128)(2,1)}, u32[]{:S(2)}, u32[]{:S(2)}) collective-permute-start(bf16[4,2,128,1024]{3,2,1,0:T(8,128)(2,1)} %dynamic-slice_bitcast_fusion.1), channel_id=1, source_target_pairs={{0,8},{8,0},{16,24},{24,16},{32,40},{40,32},{48,56},{56,48},{64,72... | collective-permute-start | bytes 6291464 | tf_op jit(solution)/shard_map/sum_core/ppermute | solution.py:260
  10.0 13.0 %copy-start.5 = (s32[512]{0:T(512)S(1)}, s32[512]{0:T(512)}, u32[]{:S(2)}) copy-start(s32[512]{0:T(512)} %param.9) | copy-start | bytes 6148
  11.5 12.1 %collective-permute-start.9 = (bf16[4,2,128,1024]{3,2,1,0:T(8,128)(2,1)}, bf16[4,2,128,1024]{3,2,1,0:T(8,128)(2,1)S(1)}, u32[]{:S(2)}, u32[]{:S(2)}) collective-permute-start(bf16[4,2,128,1024]{3,2,1,0:T(8,128)(2,1)} %dynamic-slice_bitcast_fusion), channel_id=1, source_target_pairs={{0,8},{8,0},{16,24},{24,16},{32,40},{40,32},{48,56},{56,48},{64,72... | collective-permute-start | bytes 6291464 | tf_op jit(solution)/shard_map/sum_core/ppermute | solution.py:260
  12.0 36.6 %copy-start.6 = (s32[2]{0:T(128)S(1)}, s32[2]{0:T(128)}, u32[]{:S(2)}) copy-start(s32[2]{0:T(128)} %param.8) | copy-start | bytes 28
  17.9 16.8 %collective-permute-start.1 = (bf16[2,128,1024]{2,1,0:T(8,128)(2,1)}, bf16[2,128,1024]{2,1,0:T(8,128)(2,1)}, u32[]{:S(2)}, u32[]{:S(2)}) collective-permute-start(bf16[2,128,1024]{2,1,0:T(8,128)(2,1)} %get-tuple-element.22), channel_id=1, source_target_pairs={{0,32},{8,40},{16,48},{24,56},{32,64},{40,72},{48,80},{56,88},{64,... | collective-permute-start | bytes 1572872 | tf_op jit(solution)/shard_map/sum_x/ppermute | solution.py:268
  19.4 32.7 %collective-permute-start.2 = (bf16[2,128,1024]{2,1,0:T(8,128)(2,1)S(1)}, bf16[2,128,1024]{2,1,0:T(8,128)(2,1)}, u32[]{:S(2)}, u32[]{:S(2)}) collective-permute-start(bf16[2,128,1024]{2,1,0:T(8,128)(2,1)S(1)} %get-tuple-element.24), channel_id=1, source_target_pairs={{0,96},{8,104},{16,112},{24,120},{32,0},{40,8},{48,16},{56,24},{64... | collective-permute-start | bytes 1572872 | tf_op jit(solution)/shard_map/sum_x/ppermute | solution.py:268
  21.1 31.0 %collective-permute-start.3 = (bf16[2,128,1024]{2,1,0:T(8,128)(2,1)S(1)}, bf16[2,128,1024]{2,1,0:T(8,128)(2,1)}, u32[]{:S(2)}, u32[]{:S(2)}) collective-permute-start(bf16[2,128,1024]{2,1,0:T(8,128)(2,1)S(1)} %get-tuple-element.23), channel_id=1, source_target_pairs={{0,64},{8,72},{16,80},{24,88},{32,96},{40,104},{48,112},{56,120},{... | collective-permute-start | bytes 1572872 | tf_op jit(solution)/shard_map/sum_x/ppermute | solution.py:268
  23.6 30.6 %copy-start.4 = (s32[512]{0:T(512)}, s32[512]{0:T(512)S(1)}, u32[]{:S(2)}) copy-start(s32[512]{0:T(512)S(1)} %get-tuple-element.19) | copy-start | bytes 6148
  26.6 29.4 %collective-permute-start.10 = (bf16[2,128,1024]{2,1,0:T(8,128)(2,1)}, bf16[2,128,1024]{2,1,0:T(8,128)(2,1)}, u32[]{:S(2)}, u32[]{:S(2)}) collective-permute-start(bf16[2,128,1024]{2,1,0:T(8,128)(2,1)} %get-tuple-element.25), channel_id=1, source_target_pairs={{0,32},{8,40},{16,48},{24,56},{32,64},{40,72},{48,80},{56,88},{64,... | collective-permute-start | bytes 1572872 | tf_op jit(solution)/shard_map/sum_x/ppermute | solution.py:268
  27.1 29.7 %collective-permute-start.11 = (bf16[2,128,1024]{2,1,0:T(8,128)(2,1)}, bf16[2,128,1024]{2,1,0:T(8,128)(2,1)}, u32[]{:S(2)}, u32[]{:S(2)}) collective-permute-start(bf16[2,128,1024]{2,1,0:T(8,128)(2,1)} %get-tuple-element.27), channel_id=1, source_target_pairs={{0,96},{8,104},{16,112},{24,120},{32,0},{40,8},{48,16},{56,24},{64... | collective-permute-start | bytes 1572872 | tf_op jit(solution)/shard_map/sum_x/ppermute | solution.py:268
  34.7 33.5 %collective-permute-start.12 = (bf16[2,128,1024]{2,1,0:T(8,128)(2,1)}, bf16[2,128,1024]{2,1,0:T(8,128)(2,1)}, u32[]{:S(2)}, u32[]{:S(2)}) collective-permute-start(bf16[2,128,1024]{2,1,0:T(8,128)(2,1)} %get-tuple-element.26), channel_id=1, source_target_pairs={{0,64},{8,72},{16,80},{24,88},{32,96},{40,104},{48,112},{56,120},{... | collective-permute-start | bytes 1572872 | tf_op jit(solution)/shard_map/sum_x/ppermute | solution.py:268
  54.3 17.6 %collective-permute-start.4 = (bf16[128,1024]{1,0:T(8,128)(2,1)S(1)}, bf16[128,1024]{1,0:T(8,128)(2,1)S(1)}, u32[]{:S(2)}, u32[]{:S(2)}) collective-permute-start(bf16[128,1024]{1,0:T(8,128)(2,1)S(1)} %fusion.8), channel_id=1, source_target_pairs={{0,16},{8,24},{16,0},{24,8},{32,48},{40,56},{48,32},{56,40},{64,80... | collective-permute-start | bytes 786440 | tf_op jit(solution)/shard_map/sum_y/ppermute | solution.py:273
  70.2 9.3 %collective-permute-start.13 = (bf16[128,1024]{1,0:T(8,128)(2,1)S(1)}, bf16[128,1024]{1,0:T(8,128)(2,1)S(1)}, u32[]{:S(2)}, u32[]{:S(2)}) collective-permute-start(bf16[128,1024]{1,0:T(8,128)(2,1)S(1)} %fusion.9), channel_id=1, source_target_pairs={{0,16},{8,24},{16,0},{24,8},{32,48},{40,56},{48,32},{56,40},{64,80... | collective-permute-start | bytes 786440 | tf_op jit(solution)/shard_map/sum_y/ppermute | solution.py:273
  72.3 15.2 %collective-permute-start.5 = (bf16[128,1024]{1,0:T(8,128)(2,1)S(1)}, bf16[128,1024]{1,0:T(8,128)(2,1)S(1)}, u32[]{:S(2)}, u32[]{:S(2)}) collective-permute-start(bf16[128,1024]{1,0:T(8,128)(2,1)S(1)} %multiply_convert_fusion.1), channel_id=1, source_target_pairs={{0,1},{1,0},{2,3},{3,2},{4,5},{5,4},{6,7},{7,6},{8,9},{9,8},{10,11... | collective-permute-start | bytes 786440 | tf_op jit(solution)/shard_map/gather/ppermute | solution.py:295
  80.0 26.0 %collective-permute-start.14 = (bf16[128,1024]{1,0:T(8,128)(2,1)S(1)}, bf16[128,1024]{1,0:T(8,128)(2,1)S(1)}, u32[]{:S(2)}, u32[]{:S(2)}) collective-permute-start(bf16[128,1024]{1,0:T(8,128)(2,1)S(1)} %multiply_convert_fusion), channel_id=1, source_target_pairs={{0,1},{1,0},{2,3},{3,2},{4,5},{5,4},{6,7},{7,6},{8,9},{9,8},{10,11... | collective-permute-start | bytes 786440 | tf_op jit(solution)/shard_map/gather/ppermute | solution.py:295
  87.6 18.4 %copy-start.1 = (bf16[2,128,1024]{2,1,0:T(8,128)(2,1)}, bf16[2,128,1024]{2,1,0:T(8,128)(2,1)S(1)}, u32[]{:S(2)}) copy-start(bf16[2,128,1024]{2,1,0:T(8,128)(2,1)S(1)} %pad_maximum_fusion.refs_0_) | copy-start | bytes 1572868
  87.6 21.7 %collective-permute-start.6 = (bf16[2,128,1024]{2,1,0:T(8,128)(2,1)S(1)}, bf16[2,128,1024]{2,1,0:T(8,128)(2,1)S(1)}, u32[]{:S(2)}, u32[]{:S(2)}) collective-permute-start(bf16[2,128,1024]{2,1,0:T(8,128)(2,1)S(1)} %pad_maximum_fusion.refs_0_), channel_id=1, source_target_pairs={{0,2},{1,3},{2,4},{3,5},{4,6},{5,7},{6,0},{7,1},{8,10},{9,11},{10,... | collective-permute-start | bytes 1572872 | tf_op jit(solution)/shard_map/gather/ppermute | solution.py:298
  89.6 20.3 %collective-permute-start.7 = (bf16[2,128,1024]{2,1,0:T(8,128)(2,1)S(1)}, bf16[2,128,1024]{2,1,0:T(8,128)(2,1)S(1)}, u32[]{:S(2)}, u32[]{:S(2)}) collective-permute-start(bf16[2,128,1024]{2,1,0:T(8,128)(2,1)S(1)} %pad_maximum_fusion.refs_0_), channel_id=1, source_target_pairs={{0,6},{1,7},{2,0},{3,1},{4,2},{5,3},{6,4},{7,5},{8,14},{9,15},{10,... | collective-permute-start | bytes 1572872 | tf_op jit(solution)/shard_map/gather/ppermute | solution.py:298
  91.8 25.5 %collective-permute-start.8 = (bf16[2,128,1024]{2,1,0:T(8,128)(2,1)S(1)}, bf16[2,128,1024]{2,1,0:T(8,128)(2,1)S(1)}, u32[]{:S(2)}, u32[]{:S(2)}) collective-permute-start(bf16[2,128,1024]{2,1,0:T(8,128)(2,1)S(1)} %pad_maximum_fusion.refs_0_), channel_id=1, source_target_pairs={{0,4},{1,5},{2,6},{3,7},{4,0},{5,1},{6,2},{7,3},{8,12},{9,13},{10,... | collective-permute-start | bytes 1572872 | tf_op jit(solution)/shard_map/gather/ppermute | solution.py:298
  106.0 35.9 %copy-start.2 = (bf16[2,128,1024]{2,1,0:T(8,128)(2,1)}, bf16[2,128,1024]{2,1,0:T(8,128)(2,1)S(1)}, u32[]{:S(2)}) copy-start(bf16[2,128,1024]{2,1,0:T(8,128)(2,1)S(1)} %pad_maximum_fusion.1.refs_0_) | copy-start | bytes 1572868
  106.0 35.9 %collective-permute-start.15 = (bf16[2,128,1024]{2,1,0:T(8,128)(2,1)S(1)}, bf16[2,128,1024]{2,1,0:T(8,128)(2,1)S(1)}, u32[]{:S(2)}, u32[]{:S(2)}) collective-permute-start(bf16[2,128,1024]{2,1,0:T(8,128)(2,1)S(1)} %pad_maximum_fusion.1.refs_0_), channel_id=1, source_target_pairs={{0,2},{1,3},{2,4},{3,5},{4,6},{5,7},{6,0},{7,1},{8,10},{9,11},{10,... | collective-permute-start | bytes 1572872 | tf_op jit(solution)/shard_map/gather/ppermute | solution.py:298
  107.1 34.9 %collective-permute-start.16 = (bf16[2,128,1024]{2,1,0:T(8,128)(2,1)S(1)}, bf16[2,128,1024]{2,1,0:T(8,128)(2,1)S(1)}, u32[]{:S(2)}, u32[]{:S(2)}) collective-permute-start(bf16[2,128,1024]{2,1,0:T(8,128)(2,1)S(1)} %pad_maximum_fusion.1.refs_0_), channel_id=1, source_target_pairs={{0,6},{1,7},{2,0},{3,1},{4,2},{5,3},{6,4},{7,5},{8,14},{9,15},{10,... | collective-permute-start | bytes 1572872 | tf_op jit(solution)/shard_map/gather/ppermute | solution.py:298
  109.3 8.0 %copy-start.7 = (bf16[2,128,1024]{2,1,0:T(8,128)(2,1)}, bf16[2,128,1024]{2,1,0:T(8,128)(2,1)S(1)}, u32[]{:S(2)}) copy-start(bf16[2,128,1024]{2,1,0:T(8,128)(2,1)S(1)} %collective-permute-done.6.refs_1_) | copy-start | bytes 1572868
  109.3 32.6 %collective-permute-start.17 = (bf16[2,128,1024]{2,1,0:T(8,128)(2,1)S(1)}, bf16[2,128,1024]{2,1,0:T(8,128)(2,1)S(1)}, u32[]{:S(2)}, u32[]{:S(2)}) collective-permute-start(bf16[2,128,1024]{2,1,0:T(8,128)(2,1)S(1)} %pad_maximum_fusion.1.refs_0_), channel_id=1, source_target_pairs={{0,4},{1,5},{2,6},{3,7},{4,0},{5,1},{6,2},{7,3},{8,12},{9,13},{10,... | collective-permute-start | bytes 1572872 | tf_op jit(solution)/shard_map/gather/ppermute | solution.py:298
  109.9 7.4 %copy-start.9 = (bf16[2,128,1024]{2,1,0:T(8,128)(2,1)}, bf16[2,128,1024]{2,1,0:T(8,128)(2,1)S(1)}, u32[]{:S(2)}) copy-start(bf16[2,128,1024]{2,1,0:T(8,128)(2,1)S(1)} %collective-permute-done.7.refs_2_) | copy-start | bytes 1572868
  117.3 0.9 copy-start.11
  142.0 0.8 copy-start.8
  142.0 1.0 copy-start.10
  142.0 1.1 copy-start.12
  143.1 23.8 %copy-start.3 = (bf16[128,1024]{1,0:T(8,128)(2,1)S(1)}, bf16[128,1024]{1,0:T(8,128)(2,1)}, u32[]{:S(2)}) copy-start(bf16[128,1024]{1,0:T(8,128)(2,1)} %get-tuple-element.12) | copy-start | bytes 786436
